TPU v7x, 32 devices: a whole 2x2x4 slice. The times are simulated.
32 devices in a mesh: dom: 16 (over z, y, core), section: 2 (over x).
Axes of the slice: x: 2, y: 2, z: 4, core: 2. Of those that a mesh axis runs over, the one named last changes fastest.
Arguments:
- feats: bfloat16 [65536, 1024], P('dom', 'section'), may hold values from -6 to 6
- tile_vals: bfloat16 [4096, 128, 128], P('dom'), may hold values from -0.1875 to 0.1875
- src_slot: int32 [4096], P('dom'), may hold values from 0 to 47, as said below
- dst_tile: int32 [4096], P('dom'), may hold values from 0 to 31
- tile_count: int32 [16], P('dom'), may hold values from 128 to 256, as said below
- send_tile: int32 [16, 48], P('dom'), may hold values from 0 to 31
- w_fwd: bfloat16 [1024, 1024], replicated, may hold values from -0.1875 to 0.1875
- b_fwd: float32 [1024], replicated, may hold values from -3 to 3
- w_inv1: bfloat16 [1024, 1024], replicated, may hold values from -0.1875 to 0.1875
- b_inv1: float32 [1024], replicated, may hold values from -3 to 3
- w_inv2: bfloat16 [1024, 1024], replicated, may hold values from -0.1875 to 0.1875
- b_inv2: float32 [1024], replicated, may hold values from -3 to 3
- target: bfloat16 [65536, 1024], P(('dom', 'section')), may hold values from -2.5 to 2.5
Outputs:
- hidden: bfloat16 [65536, 1024], P(('dom', 'section'))
- target_prev: bfloat16 [65536, 1024], P(('dom', 'section'))
Inputs may be any that keep to these rules, and one draw needn't show every extreme that they name: `src_slot`: slots are numbered by sending partition, 3 each; in each partition's list the entry i names slot number pi(i mod 48) for a permutation pi of the partition. `tile_count`: some partition's list is full.
All inputs are finite; a program needn't handle non-finite values.
Results may differ from a plain program's by a relative error of at most 0.0042.
Values may be sent and summed in bfloat16 or wider, within the bound.
A program may use at most 192 MiB of HBM per device.

v0:
```python
import jax
import jax.numpy as jnp
from jax import lax
from jax.sharding import PartitionSpec as P

BLOCK = 16


def per_device(
    feats,
    tile_vals,
    src_slot,
    dst_tile,
    tile_count,
    send_tile,
    w_fwd,
    b_fwd,
    w_inv1,
    b_inv1,
    w_inv2,
    b_inv2,
    target,
):
    node_rows, feat_cols = feats.shape
    tile_side = tile_vals.shape[1]
    row_tiles = node_rows // tile_side
    recv_count = send_tile.shape[1]
    flat_width = tile_side * feat_cols
    flat_blocks = feats.reshape(row_tiles, flat_width)
    tile_ids = jnp.arange(row_tiles, dtype=jnp.int32)
    pick_send = (send_tile[0][:, None] == tile_ids[None, :]).astype(jnp.bfloat16)
    outgoing = jnp.dot(pick_send, flat_blocks, preferred_element_type=jnp.float32).astype(
        jnp.bfloat16
    )
    received = lax.all_to_all(
        outgoing.reshape(recv_count, tile_side, feat_cols),
        "dom",
        split_axis=0,
        concat_axis=0,
        tiled=True,
    )
    received_flat = received.reshape(recv_count, flat_width)
    slot_ids = jnp.arange(recv_count, dtype=jnp.int32)
    live_count = tile_count[0]
    turns_needed = (live_count + BLOCK - 1) // BLOCK

    def accumulate(turn_index, running):
        offset = turn_index * BLOCK
        values_block = lax.dynamic_slice_in_dim(tile_vals, offset, BLOCK, 0)
        slot_block = lax.dynamic_slice_in_dim(src_slot, offset, BLOCK, 0)
        dest_block = lax.dynamic_slice_in_dim(dst_tile, offset, BLOCK, 0)
        pick_slot = (slot_block[:, None] == slot_ids[None, :]).astype(jnp.bfloat16)
        sources = jnp.dot(pick_slot, received_flat, preferred_element_type=jnp.float32).astype(
            jnp.bfloat16
        )
        products = jnp.einsum(
            "lab,lbc->lac",
            values_block,
            sources.reshape(BLOCK, tile_side, feat_cols),
            preferred_element_type=jnp.float32,
        )
        active = offset + jnp.arange(BLOCK, dtype=jnp.int32) < live_count
        place = ((tile_ids[:, None] == dest_block[None, :]) & active[None, :]).astype(jnp.float32)
        return running + jnp.dot(
            place, products.reshape(BLOCK, flat_width), precision=lax.Precision.HIGHEST
        )

    summed = lax.fori_loop(
        0, turns_needed, accumulate, jnp.zeros((row_tiles, flat_width), jnp.float32)
    )
    agg = summed.reshape(node_rows, feat_cols).astype(jnp.bfloat16)
    agg_rows, input_rows = (
        lax.all_to_all(agg, "section", split_axis=0, concat_axis=1, tiled=True),
        lax.all_to_all(feats, "section", split_axis=0, concat_axis=1, tiled=True),
    )
    hidden = jnp.tanh(jnp.dot(agg_rows, w_fwd, preferred_element_type=jnp.float32) + b_fwd).astype(
        jnp.bfloat16
    )

    def inverse(values):
        inner = jnp.tanh(
            jnp.dot(values, w_inv1, preferred_element_type=jnp.float32) + b_inv1
        ).astype(jnp.bfloat16)
        return jnp.tanh(jnp.dot(inner, w_inv2, preferred_element_type=jnp.float32) + b_inv2)

    shifted = input_rows.astype(jnp.float32) + inverse(target) - inverse(hidden)
    return (hidden, shifted.astype(jnp.bfloat16))


def solution(mesh):
    placed = (
        P("dom", "section"),
        P("dom", None, None),
        P("dom"),
        P("dom"),
        P("dom"),
        P("dom", None),
        P(),
        P(),
        P(),
        P(),
        P(),
        P(),
        P(("dom", "section"), None),
    )
    return jax.shard_map(
        per_device,
        mesh=mesh,
        in_specs=placed,
        out_specs=(P(("dom", "section"), None), P(("dom", "section"), None)),
        check_vma=False,
    )
```

profile of v0, /device:TPU:9, one launch (start us, length us, event | category | flops | bytes accessed | tf_op | source)
XLA Modules:
  0.0 533.6 jit_solution(18329479635063914049)
XLA Ops:
  0.7 5.8 %reshape.43 = bf16[32,65536]{1,0:T(8,128)(2,1)} reshape(bf16[4096,512]{1,0:T(8,128)(2,1)} %param.15) | data formatting | bytes 8388608 | tf_op jit(solution)/shard_map/reshape | solution.py:29
  6.4 4.0 convolution_convert_fusion.1
  10.4 5.0 copy.24
  15.5 6.6 %all-to-all-start = ((bf16[48,128,512]{2,1,0:T(8,128)(2,1)}), bf16[48,128,512]{2,1,0:T(8,128)(2,1)}, u32[]{:S(2)}, u32[]{:S(2)}) async-start(bf16[48,128,512]{2,1,0:T(8,128)(2,1)} %bitcast.49), calls=%async_computation | async-start | bytes 12582912 | tf_op jit(solution)/shard_map/all_to_all | solution.py:35
  22.8 134.6 %all-to-all-done = bf16[48,128,512]{2,1,0:T(8,128)(2,1)} async-done(((bf16[48,128,512]{2,1,0:T(8,128)(2,1)}), bf16[48,128,512]{2,1,0:T(8,128)(2,1)}, u32[]{:S(2)}, u32[]{:S(2)}) %all-to-all-start) | async-done | bytes 6291488 | tf_op jit(solution)/shard_map/all_to_all | solution.py:35
  157.3 5.6 %all-to-all-start.2 = ((bf16[2,2048,512]{2,1,0:T(8,128)(2,1)}), bf16[2,2048,512]{2,1,0:T(8,128)(2,1)}, u32[]{:S(2)}, u32[]{:S(2)}) async-start(bf16[2,2048,512]{2,1,0:T(8,128)(2,1)} %bitcast.51), calls=%async_computation.2 | async-start | bytes 8388608 | tf_op jit(solution)/shard_map/all_to_all | solution.py:74
  162.9 9.2 %copy.25 = bf16[6,8,128,512]{3,1,2,0:T(8,128)(2,1)} copy(bf16[6,8,128,512]{3,2,1,0:T(8,128)(2,1)} %bitcast.14) | data formatting | bytes 12582912
  172.1 3.8 broadcast_in_dim.2
  175.9 261.0 %while.11 = (s32[]{:T(128)}, f32[32,65536]{1,0:T(8,128)}, s32[]{:T(128)}, s32[256]{0:T(256)S(1)}, s32[]{:T(128)}, /*index=5*/bf16[256,128,128]{2,1,0:T(8,128)(2,...) while((s32[]{:T(128)}, f32[32,65536]{1,0:T(8,128)}, ...), condition=%wide.region_1.2_spmd.clone, body=%wide.region_0.1_spmd.clone.sunk | while | flops 774899456 | bytes 48759384 | solution.py:68
  176.0 3.8 convolution_convert_fusion.3
  182.2 2.4 copy.29
  185.4 7.9 %convolution_add_fusion.2 = f32[32,65536]{1,0:T(8,128)} fusion(f32[32,65536]{1,0:T(8,128)} %get-tuple-element.155, f32[16,65536]{1,0:T(8,128)S(1)} %bitcast.45, s32[16]{0:T(128)S(1)} %dynamic_slice.19, pred[16]{0:T(512)(128)(4,1)S(1)} %add_compare_fusion.2), kind=kOutput, calls=%fused_computation.2.clone.1 | convolution fusion | flops 404751360 | bytes 20971600 | tf_op jit(solution)/shard_map/while/body/dot_general | solution.py:64
  193.4 3.8 convolution_convert_fusion.3
  199.6 2.4 copy.29
  202.8 7.9 %convolution_add_fusion.2 = f32[32,65536]{1,0:T(8,128)} fusion(f32[32,65536]{1,0:T(8,128)} %get-tuple-element.155, f32[16,65536]{1,0:T(8,128)S(1)} %bitcast.45, s32[16]{0:T(128)S(1)} %dynamic_slice.19, pred[16]{0:T(512)(128)(4,1)S(1)} %add_compare_fusion.2), kind=kOutput, calls=%fused_computation.2.clone.1 | convolution fusion | flops 404751360 | bytes 20971600 | tf_op jit(solution)/shard_map/while/body/dot_general | solution.py:64
  210.8 3.8 convolution_convert_fusion.3
  217.0 2.4 copy.29
  220.2 7.9 %convolution_add_fusion.2 = f32[32,65536]{1,0:T(8,128)} fusion(f32[32,65536]{1,0:T(8,128)} %get-tuple-element.155, f32[16,65536]{1,0:T(8,128)S(1)} %bitcast.45, s32[16]{0:T(128)S(1)} %dynamic_slice.19, pred[16]{0:T(512)(128)(4,1)S(1)} %add_compare_fusion.2), kind=kOutput, calls=%fused_computation.2.clone.1 | convolution fusion | flops 404751360 | bytes 20971600 | tf_op jit(solution)/shard_map/while/body/dot_general | solution.py:64
  228.2 3.8 convolution_convert_fusion.3
  234.4 2.4 copy.29
  237.6 7.9 %convolution_add_fusion.2 = f32[32,65536]{1,0:T(8,128)} fusion(f32[32,65536]{1,0:T(8,128)} %get-tuple-element.155, f32[16,65536]{1,0:T(8,128)S(1)} %bitcast.45, s32[16]{0:T(128)S(1)} %dynamic_slice.19, pred[16]{0:T(512)(128)(4,1)S(1)} %add_compare_fusion.2), kind=kOutput, calls=%fused_computation.2.clone.1 | convolution fusion | flops 404751360 | bytes 20971600 | tf_op jit(solution)/shard_map/while/body/dot_general | solution.py:64
  245.6 3.8 convolution_convert_fusion.3
  251.8 2.4 copy.29
  255.0 7.9 %convolution_add_fusion.2 = f32[32,65536]{1,0:T(8,128)} fusion(f32[32,65536]{1,0:T(8,128)} %get-tuple-element.155, f32[16,65536]{1,0:T(8,128)S(1)} %bitcast.45, s32[16]{0:T(128)S(1)} %dynamic_slice.19, pred[16]{0:T(512)(128)(4,1)S(1)} %add_compare_fusion.2), kind=kOutput, calls=%fused_computation.2.clone.1 | convolution fusion | flops 404751360 | bytes 20971600 | tf_op jit(solution)/shard_map/while/body/dot_general | solution.py:64
  263.0 3.8 convolution_convert_fusion.3
  269.2 2.4 copy.29
  272.4 7.9 %convolution_add_fusion.2 = f32[32,65536]{1,0:T(8,128)} fusion(f32[32,65536]{1,0:T(8,128)} %get-tuple-element.155, f32[16,65536]{1,0:T(8,128)S(1)} %bitcast.45, s32[16]{0:T(128)S(1)} %dynamic_slice.19, pred[16]{0:T(512)(128)(4,1)S(1)} %add_compare_fusion.2), kind=kOutput, calls=%fused_computation.2.clone.1 | convolution fusion | flops 404751360 | bytes 20971600 | tf_op jit(solution)/shard_map/while/body/dot_general | solution.py:64
  280.4 3.8 convolution_convert_fusion.3
  286.6 2.4 copy.29
  289.8 7.9 %convolution_add_fusion.2 = f32[32,65536]{1,0:T(8,128)} fusion(f32[32,65536]{1,0:T(8,128)} %get-tuple-element.155, f32[16,65536]{1,0:T(8,128)S(1)} %bitcast.45, s32[16]{0:T(128)S(1)} %dynamic_slice.19, pred[16]{0:T(512)(128)(4,1)S(1)} %add_compare_fusion.2), kind=kOutput, calls=%fused_computation.2.clone.1 | convolution fusion | flops 404751360 | bytes 20971600 | tf_op jit(solution)/shard_map/while/body/dot_general | solution.py:64
  297.8 3.8 convolution_convert_fusion.3
  304.0 2.4 copy.29
  307.2 7.9 %convolution_add_fusion.2 = f32[32,65536]{1,0:T(8,128)} fusion(f32[32,65536]{1,0:T(8,128)} %get-tuple-element.155, f32[16,65536]{1,0:T(8,128)S(1)} %bitcast.45, s32[16]{0:T(128)S(1)} %dynamic_slice.19, pred[16]{0:T(512)(128)(4,1)S(1)} %add_compare_fusion.2), kind=kOutput, calls=%fused_computation.2.clone.1 | convolution fusion | flops 404751360 | bytes 20971600 | tf_op jit(solution)/shard_map/while/body/dot_general | solution.py:64
  315.2 3.8 convolution_convert_fusion.3
  321.4 2.4 copy.29
  324.6 7.9 %convolution_add_fusion.2 = f32[32,65536]{1,0:T(8,128)} fusion(f32[32,65536]{1,0:T(8,128)} %get-tuple-element.155, f32[16,65536]{1,0:T(8,128)S(1)} %bitcast.45, s32[16]{0:T(128)S(1)} %dynamic_slice.19, pred[16]{0:T(512)(128)(4,1)S(1)} %add_compare_fusion.2), kind=kOutput, calls=%fused_computation.2.clone.1 | convolution fusion | flops 404751360 | bytes 20971600 | tf_op jit(solution)/shard_map/while/body/dot_general | solution.py:64
  332.6 3.8 convolution_convert_fusion.3
  338.8 2.4 copy.29
  342.0 7.9 %convolution_add_fusion.2 = f32[32,65536]{1,0:T(8,128)} fusion(f32[32,65536]{1,0:T(8,128)} %get-tuple-element.155, f32[16,65536]{1,0:T(8,128)S(1)} %bitcast.45, s32[16]{0:T(128)S(1)} %dynamic_slice.19, pred[16]{0:T(512)(128)(4,1)S(1)} %add_compare_fusion.2), kind=kOutput, calls=%fused_computation.2.clone.1 | convolution fusion | flops 404751360 | bytes 20971600 | tf_op jit(solution)/shard_map/while/body/dot_general | solution.py:64
  350.0 3.8 convolution_convert_fusion.3
  356.2 2.4 copy.29
  359.4 7.9 %convolution_add_fusion.2 = f32[32,65536]{1,0:T(8,128)} fusion(f32[32,65536]{1,0:T(8,128)} %get-tuple-element.155, f32[16,65536]{1,0:T(8,128)S(1)} %bitcast.45, s32[16]{0:T(128)S(1)} %dynamic_slice.19, pred[16]{0:T(512)(128)(4,1)S(1)} %add_compare_fusion.2), kind=kOutput, calls=%fused_computation.2.clone.1 | convolution fusion | flops 404751360 | bytes 20971600 | tf_op jit(solution)/shard_map/while/body/dot_general | solution.py:64
  367.4 3.8 convolution_convert_fusion.3
  373.6 2.4 copy.29
  376.8 7.9 %convolution_add_fusion.2 = f32[32,65536]{1,0:T(8,128)} fusion(f32[32,65536]{1,0:T(8,128)} %get-tuple-element.155, f32[16,65536]{1,0:T(8,128)S(1)} %bitcast.45, s32[16]{0:T(128)S(1)} %dynamic_slice.19, pred[16]{0:T(512)(128)(4,1)S(1)} %add_compare_fusion.2), kind=kOutput, calls=%fused_computation.2.clone.1 | convolution fusion | flops 404751360 | bytes 20971600 | tf_op jit(solution)/shard_map/while/body/dot_general | solution.py:64
  384.8 3.8 convolution_convert_fusion.3
  391.0 2.4 copy.29
  394.2 7.9 %convolution_add_fusion.2 = f32[32,65536]{1,0:T(8,128)} fusion(f32[32,65536]{1,0:T(8,128)} %get-tuple-element.155, f32[16,65536]{1,0:T(8,128)S(1)} %bitcast.45, s32[16]{0:T(128)S(1)} %dynamic_slice.19, pred[16]{0:T(512)(128)(4,1)S(1)} %add_compare_fusion.2), kind=kOutput, calls=%fused_computation.2.clone.1 | convolution fusion | flops 404751360 | bytes 20971600 | tf_op jit(solution)/shard_map/while/body/dot_general | solution.py:64
  402.2 3.8 convolution_convert_fusion.3
  408.4 2.4 copy.29
  411.6 7.9 %convolution_add_fusion.2 = f32[32,65536]{1,0:T(8,128)} fusion(f32[32,65536]{1,0:T(8,128)} %get-tuple-element.155, f32[16,65536]{1,0:T(8,128)S(1)} %bitcast.45, s32[16]{0:T(128)S(1)} %dynamic_slice.19, pred[16]{0:T(512)(128)(4,1)S(1)} %add_compare_fusion.2), kind=kOutput, calls=%fused_computation.2.clone.1 | convolution fusion | flops 404751360 | bytes 20971600 | tf_op jit(solution)/shard_map/while/body/dot_general | solution.py:64
  419.6 3.8 convolution_convert_fusion.3
  425.8 2.4 copy.29
  429.0 7.9 %convolution_add_fusion.2 = f32[32,65536]{1,0:T(8,128)} fusion(f32[32,65536]{1,0:T(8,128)} %get-tuple-element.155, f32[16,65536]{1,0:T(8,128)S(1)} %bitcast.45, s32[16]{0:T(128)S(1)} %dynamic_slice.19, pred[16]{0:T(512)(128)(4,1)S(1)} %add_compare_fusion.2), kind=kOutput, calls=%fused_computation.2.clone.1 | convolution fusion | flops 404751360 | bytes 20971600 | tf_op jit(solution)/shard_map/while/body/dot_general | solution.py:64
  436.9 5.8 %convert_element_type.38 = bf16[32,65536]{1,0:T(8,128)(2,1)} convert(f32[32,65536]{1,0:T(8,128)} %get-tuple-element.55) | non-fusion elementwise | flops 2097152 | bytes 12582912 | tf_op jit(solution)/shard_map/convert_element_type | solution.py:71
  442.7 5.6 %convert_element_type.39 = bf16[2,2048,512]{2,1,0:T(8,128)(2,1)} reshape(bf16[32,65536]{1,0:T(8,128)(2,1)} %convert_element_type.38) | data formatting | bytes 8388608 | tf_op jit(solution)/shard_map/convert_element_type | solution.py:71
  448.3 5.9 %all-to-all-start.1 = ((bf16[2,2048,512]{2,1,0:T(8,128)(2,1)}), bf16[2,2048,512]{2,1,0:T(8,128)(2,1)}, u32[]{:S(2)}, u32[]{:S(2)}) async-start(bf16[2,2048,512]{2,1,0:T(8,128)(2,1)} %convert_element_type.39), calls=%async_computation.1 | async-start | bytes 8388608 | tf_op jit(solution)/shard_map/all_to_all | solution.py:73
  454.3 13.2 %fusion.12 = f32[2048,1024]{1,0:T(8,128)} fusion(bf16[1024,1024]{1,0:T(8,128)(2,1)S(1)} %copy-done, f32[1024]{0:T(1024)S(1)} %copy-done.3, bf16[2048,1024]{1,0:T(8,128)(2,1)} %param.27, bf16[1024,1024]{1,0:T(8,128)(2,1)} %param.23), kind=kOutput, calls=%fused_computation.20 | convolution fusion | flops 8594128896 | bytes 16781312 | tf_op jit(solution)/shard_map/dot_general | solution.py:84
  467.5 3.4 convert_bitcast_fusion
  470.9 4.3 copy.23
  475.1 26.0 %all-to-all-done.1 = bf16[2,2048,512]{2,1,0:T(8,128)(2,1)} async-done(((bf16[2,2048,512]{2,1,0:T(8,128)(2,1)}), bf16[2,2048,512]{2,1,0:T(8,128)(2,1)}, u32[]{:S(2)}, u32[]{:S(2)}) %all-to-all-start.1) | async-done | bytes 4194336 | tf_op jit(solution)/shard_map/all_to_all | solution.py:73
  501.1 6.2 %copy.19 = bf16[2048,2,512]{0,2,1:T(8,128)(2,1)} copy(bf16[2048,2,512]{2,0,1:T(8,128)(2,1)} %bitcast.2) | data formatting | bytes 8388608 | tf_op jit(solution)/shard_map/all_to_all | solution.py:73
  507.3 9.5 %tanh_convert_fusion.2 = bf16[2048,1024]{1,0:T(8,128)(2,1)} fusion(f32[1024]{0:T(1024)S(1)} %copy-done.2, bf16[2048,1024]{0,1:T(8,128)(2,1)} %bitcast.53, bf16[1024,1024]{1,0:T(8,128)(2,1)} %param.21), kind=kOutput, calls=%fused_computation.19 | convolution fusion | flops 4299161600 | bytes 10489856 | tf_op jit(solution)/shard_map/dot_general | solution.py:76
  516.8 16.7 %subtract_convert_fusion = bf16[2048,1024]{1,0:T(8,128)(2,1)} fusion(f32[2048,1024]{1,0:T(8,128)} %bitcast.52, f32[2048,1024]{1,0:T(8,128)} %fusion.12, f32[1024]{0:T(1024)S(1)} %copy-done.4, bf16[1024,1024]{1,0:T(8,128)(2,1)S(1)} %copy-done, f32[1024]{0:T(1024)S(1)} %copy-done.3, bf16[2048,1024]{1,0:T(8,128)(2,1)} %tanh_convert_fusion.2, ...), kind=kOutput, calls=%fused_computation.16 | convolution fusion | flops 8604614656 | bytes 29368320 | tf_op jit(solution)/shard_map/dot_general | solution.py:84
  (90 shorter events, 48.3 us)
Async XLA Ops:
  0.6 453.6 %copy-start = (bf16[1024,1024]{1,0:T(8,128)(2,1)S(1)}, bf16[1024,1024]{1,0:T(8,128)(2,1)}, u32[]{:S(2)}) copy-start(bf16[1024,1024]{1,0:T(8,128)(2,1)} %param.25) | copy-start | bytes 6291460
  0.6 5.8 %copy-start.1 = (s32[1,48]{1,0:T(1,128)S(1)}, s32[1,48]{1,0:T(1,128)}, u32[]{:S(2)}) copy-start(s32[1,48]{1,0:T(1,128)} %param.20) | copy-start | bytes 580
  15.5 141.9 %all-to-all-start = ((bf16[48,128,512]{2,1,0:T(8,128)(2,1)}), bf16[48,128,512]{2,1,0:T(8,128)(2,1)}, u32[]{:S(2)}, u32[]{:S(2)}) async-start(bf16[48,128,512]{2,1,0:T(8,128)(2,1)} %bitcast.49), calls=%async_computation | async-start | bytes 12582912 | tf_op jit(solution)/shard_map/all_to_all | solution.py:35
  157.3 291.0 %all-to-all-start.2 = ((bf16[2,2048,512]{2,1,0:T(8,128)(2,1)}), bf16[2,2048,512]{2,1,0:T(8,128)(2,1)}, u32[]{:S(2)}, u32[]{:S(2)}) async-start(bf16[2,2048,512]{2,1,0:T(8,128)(2,1)} %bitcast.51), calls=%async_computation.2 | async-start | bytes 8388608 | tf_op jit(solution)/shard_map/all_to_all | solution.py:74
  172.1 3.8 copy-start.5
  172.1 3.8 copy-start.6
  448.3 6.0 %copy-start.3 = (f32[1024]{0:T(1024)S(1)}, f32[1024]{0:T(1024)}, u32[]{:S(2)}) copy-start(f32[1024]{0:T(1024)} %param.24) | copy-start | bytes 12292
  448.3 52.8 %all-to-all-start.1 = ((bf16[2,2048,512]{2,1,0:T(8,128)(2,1)}), bf16[2,2048,512]{2,1,0:T(8,128)(2,1)}, u32[]{:S(2)}, u32[]{:S(2)}) async-start(bf16[2,2048,512]{2,1,0:T(8,128)(2,1)} %convert_element_type.39), calls=%async_computation.1 | async-start | bytes 8388608 | tf_op jit(solution)/shard_map/all_to_all | solution.py:73
  501.1 6.2 %copy-start.2 = (f32[1024]{0:T(1024)S(1)}, f32[1024]{0:T(1024)}, u32[]{:S(2)}) copy-start(f32[1024]{0:T(1024)} %param.22) | copy-start | bytes 12292
  507.3 9.5 %copy-start.4 = (f32[1024]{0:T(1024)S(1)}, f32[1024]{0:T(1024)}, u32[]{:S(2)}) copy-start(f32[1024]{0:T(1024)} %param.26) | copy-start | bytes 12292
where the time goes:
time: 536 us; the launch traced here: 534 us
  matrix products  245 us (46%)
  waiting for transfers between devices  161 us (30%)
  local copies, waits for them, and re-layouts  88.9 us (17%)
  other arithmetic  18.9 us (4%)
  starting transfers between devices  18.1 us (3%)
    all_to_all x1, waiting for transfers between devices, per_device(): lax.all_to_all(outgoing.reshape(recv_count, tile_side, feat_cols), 'dom',...  135 us
    dot_general x15, matrix products, accumulate(): jnp.dot(place, products.reshape(BLOCK, flat_width), precision=lax.Precisi...  119 us
    dot_general x15, matrix products, accumulate(): jnp.dot(pick_slot, received_flat, preferred_element_type=jnp.float32)  56.7 us
    while x30, local copies, waits for them, and re-layouts  46.7 us
    dot_general x2, matrix products, inverse(): jnp.dot(inner, w_inv2, preferred_element_type=jnp.float32) + b_inv2  30 us
    dot_general x15, matrix products, accumulate(): jnp.einsum('lab,lbc->lac', values_block, sources.reshape(BLOCK, tile_side...  26 us
    all_to_all x1, waiting for transfers between devices, per_device(): lax.all_to_all(agg, 'section', split_axis=0, concat_axis=1, tiled=True)  26 us
    unnamed x16, local copies, waits for them, and re-layouts  14.3 us
  transfers between devices with their start and end apart: 3, of which 2 were waited for; matrix products, arithmetic and copies ran while one was open for 57% of the time, Pallas kernels for 0%

commit v1 on v0

v1 whole, which is shorter than its diff:
```python
import functools

import jax
import jax.numpy as jnp
from jax import lax
from jax.experimental import pallas as pl
from jax.experimental.pallas import tpu as pltpu
from jax.sharding import PartitionSpec as P

MESH = pl.DeviceIdType.MESH
BF16 = jnp.bfloat16
F32 = jnp.float32


def plan_kernel(steps, row_tiles, count_ref, dst_ref, slot_ref, plan_ref):
    entries = dst_ref.shape[1]
    width = plan_ref.shape[1]
    lane = lax.broadcasted_iota(jnp.int32, (entries, entries), 1)
    sub = lax.broadcasted_iota(jnp.int32, (entries, entries), 0)
    live = lax.broadcasted_iota(jnp.int32, (1, entries), 1) < count_ref[0]
    key_row = jnp.where(live, dst_ref[...], row_tiles).astype(F32)
    eye = lane == sub

    def column(row):
        return jnp.sum(jnp.where(eye, row, 0.0), axis=1, keepdims=True)

    key_col = column(key_row)
    slot_col = column(slot_ref[...].astype(F32))
    rank = jnp.sum(jnp.where((key_row == key_col) & (lane < sub), 1.0, 0.0), axis=1, keepdims=True)
    tile_lane = lax.broadcasted_iota(jnp.int32, (entries, width), 1).astype(F32)
    tile_sub = lax.broadcasted_iota(jnp.int32, (width, entries), 0).astype(F32)
    n_row = jnp.sum(jnp.where(key_col == tile_lane, 1.0, 0.0), axis=0, keepdims=True)
    n_col = jnp.sum(jnp.where(key_row == tile_sub, 1.0, 0.0), axis=1, keepdims=True)
    r_row = lax.broadcasted_iota(jnp.int32, (1, width), 1).astype(F32)
    r_col = lax.broadcasted_iota(jnp.int32, (width, 1), 0).astype(F32)
    pairs_row = jnp.where(r_row < row_tiles, jnp.floor((n_row + 1.0) * 0.5), 0.0)
    pairs_col = jnp.where(r_col < row_tiles, jnp.floor((n_col + 1.0) * 0.5), 0.0)
    big_lane = lax.broadcasted_iota(jnp.int32, (width, width), 1).astype(F32)
    big_sub = lax.broadcasted_iota(jnp.int32, (width, width), 0).astype(F32)
    start_row = jnp.sum(jnp.where(big_sub < big_lane, pairs_col, 0.0), axis=0, keepdims=True)
    start_col = jnp.sum(jnp.where(big_lane < big_sub, pairs_row, 0.0), axis=1, keepdims=True)
    start_of = jnp.sum(jnp.where(tile_lane < key_col, pairs_row, 0.0), axis=1, keepdims=True)
    place = jnp.where(key_col < row_tiles, 2.0 * start_of + rank, -1.0)
    entry_col = lax.broadcasted_iota(jnp.int32, (entries, 1), 0).astype(F32)
    for half in range(2):
        hit = place == 2.0 * tile_lane + float(half)
        found = jnp.sum(jnp.where(hit, 1.0, 0.0), axis=0, keepdims=True)
        entry = jnp.sum(jnp.where(hit, entry_col, 0.0), axis=0, keepdims=True)
        entry = entry + (1.0 - found) * float(entries)
        slot = jnp.sum(jnp.where(hit, slot_col, 0.0), axis=0, keepdims=True)
        plan_ref[half : half + 1, :] = entry.astype(jnp.int32)
        plan_ref[2 + half : 3 + half, :] = slot.astype(jnp.int32)
    opens = jnp.sum(
        jnp.where((start_col == big_lane) & (pairs_col > 0.0), 1.0, 0.0), axis=0, keepdims=True
    )
    plan_ref[4:5, :] = (1.0 - opens).astype(jnp.int32)
    last = jnp.where(pairs_row > 0.0, start_row + pairs_row - 1.0, float(steps))
    plan_ref[5:6, :] = last.astype(jnp.int32)
    plan_ref[6:8, :] = jnp.zeros((2, width), jnp.int32)


def layer_kernel(
    cfg,
    send_tile,
    plan,
    feats_hbm,
    vals_hbm,
    target_hbm,
    w_fwd_hbm,
    w_inv1_hbm,
    w_inv2_hbm,
    b_fwd,
    b_inv1,
    b_inv2,
    hidden_hbm,
    prev_hbm,
    feats,
    vals,
    target,
    w_fwd,
    w_inv1,
    w_inv2,
    whole_feats,
    base,
    agg,
    agg_out,
    sums,
    load_sem,
    out_sem,
    dom_send,
    dom_recv,
    feat_send,
    feat_recv,
    agg_send,
    agg_recv,
    *chunk_bufs,
):
    n, n_sec, slots, chunks, width, steps, group = cfg
    outgoing, received = chunk_bufs[:chunks], chunk_bufs[chunks:]
    me = lax.axis_index("dom")
    sec = lax.axis_index("section")
    row_tiles, side, cols = feats.shape
    own_tiles = row_tiles // n_sec
    groups = own_tiles // group
    entries = vals_hbm.shape[0]
    d = agg.shape[2]
    my_cols = pl.multiple_of(sec * cols, 128)

    loads = [
        pltpu.make_async_copy(feats_hbm, feats, load_sem.at[0]),
        pltpu.make_async_copy(target_hbm, target, load_sem.at[1]),
        pltpu.make_async_copy(w_inv1_hbm, w_inv1, load_sem.at[2]),
        pltpu.make_async_copy(w_inv2_hbm, w_inv2, load_sem.at[3]),
        pltpu.make_async_copy(vals_hbm, vals.at[pl.ds(0, entries)], load_sem.at[4]),
        pltpu.make_async_copy(w_fwd_hbm, w_fwd, load_sem.at[5]),
    ]
    for load in loads:
        load.start()

    barrier = pltpu.get_barrier_semaphore()

    def greet_dom(i, _):
        pl.semaphore_signal(
            barrier, inc=1, device_id=(lax.rem(me + i, n), sec), device_id_type=MESH
        )
        return 0

    def greet_sec(i, _):
        pl.semaphore_signal(
            barrier, inc=1, device_id=(me, lax.rem(sec + i, n_sec)), device_id_type=MESH
        )
        return 0

    lax.fori_loop(1, n, greet_dom, 0)
    lax.fori_loop(1, n_sec, greet_sec, 0)

    def offset(i):
        return n // 2 + (1 - 2 * lax.rem(i, 2)) * ((i + 1) // 2)

    def dom_copy(c, i):
        far = offset(i)
        return pltpu.make_async_remote_copy(
            src_ref=outgoing[c].at[pl.ds(i * slots, slots)],
            dst_ref=received[c].at[pl.ds(me * slots, slots)],
            send_sem=dom_send.at[c, i],
            recv_sem=dom_recv.at[c, i],
            device_id=(lax.rem(me + far, n), sec),
            device_id_type=MESH,
        )

    def dom_arrival(c, i):
        source = lax.rem(me + n - offset(i), n)
        return pltpu.make_async_remote_copy(
            src_ref=outgoing[c].at[pl.ds(i * slots, slots)],
            dst_ref=received[c].at[pl.ds(source * slots, slots)],
            send_sem=dom_send.at[c, i],
            recv_sem=dom_recv.at[c, i],
            device_id=(source, sec),
            device_id_type=MESH,
        )

    def feat_copy(i):
        other = lax.rem(sec + i, n_sec)
        return pltpu.make_async_remote_copy(
            src_ref=feats.at[pl.ds(other * own_tiles, own_tiles)],
            dst_ref=whole_feats.at[:, :, pl.ds(my_cols, cols)],
            send_sem=feat_send.at[i],
            recv_sem=feat_recv.at[i],
            device_id=(me, other),
            device_id_type=MESH,
        )

    def feat_arrival(i):
        source = lax.rem(sec + n_sec - i, n_sec)
        return pltpu.make_async_remote_copy(
            src_ref=feats.at[pl.ds(source * own_tiles, own_tiles)],
            dst_ref=whole_feats.at[:, :, pl.ds(pl.multiple_of(source * cols, 128), cols)],
            send_sem=feat_send.at[i],
            recv_sem=feat_recv.at[i],
            device_id=(me, source),
            device_id_type=MESH,
        )

    def agg_copy(c, i, b):
        other = lax.rem(sec + i, n_sec)
        return pltpu.make_async_remote_copy(
            src_ref=agg_out.at[c, i - 1, pl.ds(b * group, group)],
            dst_ref=agg.at[
                pl.ds(b * group, group),
                :,
                pl.ds(pl.multiple_of(my_cols + c * width, 128), width),
            ],
            send_sem=agg_send.at[c, i, b],
            recv_sem=agg_recv.at[c, i, b],
            device_id=(me, other),
            device_id_type=MESH,
        )

    def agg_arrival(c, i, b):
        source = lax.rem(sec + n_sec - i, n_sec)
        return pltpu.make_async_remote_copy(
            src_ref=agg_out.at[c, i - 1, pl.ds(b * group, group)],
            dst_ref=agg.at[
                pl.ds(b * group, group),
                :,
                pl.ds(pl.multiple_of(source * cols + c * width, 128), width),
            ],
            send_sem=agg_send.at[c, i, b],
            recv_sem=agg_recv.at[c, i, b],
            device_id=(me, source),
            device_id_type=MESH,
        )

    loads[0].wait()
    own_feats = pltpu.make_async_copy(
        feats.at[pl.ds(sec * own_tiles, own_tiles)],
        whole_feats.at[:, :, pl.ds(my_cols, cols)],
        load_sem.at[6],
    )
    own_feats.start()
    for c in range(chunks):
        left = slice(c * width, (c + 1) * width)

        def gather(i, _):
            first = lax.rem(me + offset(i), n) * slots
            for k in range(slots):
                outgoing[c][i * slots + k] = feats[send_tile[0, first + k], :, left]
            return 0

        lax.fori_loop(0, n - 1, gather, 0)
        for k in range(slots):
            received[c][me * slots + k] = feats[send_tile[0, me * slots + k], :, left]
        if c == 0:
            pl.semaphore_wait(barrier, n + n_sec - 2)

        def send(i, _):
            dom_copy(c, i).start()
            return 0

        lax.fori_loop(0, n - 1, send, 0)

    def send_feat(i, _):
        feat_copy(i).start()
        return 0

    lax.fori_loop(1, n_sec, send_feat, 0)

    def inverse(values):
        inner = jnp.tanh(
            jnp.dot(values, w_inv1[...], preferred_element_type=F32) + b_inv1[...]
        ).astype(BF16)
        return jnp.tanh(jnp.dot(inner, w_inv2[...], preferred_element_type=F32) + b_inv2[...])

    for load in loads[1:4]:
        load.wait()

    def target_block(b, _):
        rows = pl.ds(b * group, group)
        values = target[rows].reshape(group * side, d)
        base[rows] = inverse(values).reshape(group, side, d)
        return 0

    lax.fori_loop(0, groups, target_block, 0)

    vals[entries] = jnp.zeros((side, side), BF16)
    sums[steps] = jnp.zeros((side, width), BF16)
    loads[4].wait()

    for c in range(chunks):

        def arrive(i, _):
            dom_arrival(c, i).wait_recv()
            return 0

        lax.fori_loop(0, n - 1, arrive, 0)

        def step(t, total):
            left = jnp.concatenate([vals[plan[0, t]], vals[plan[1, t]]], axis=1)
            right = jnp.concatenate(
                [received[c][plan[2, t]], received[c][plan[3, t]]], axis=0
            )
            total = total * plan[4, t].astype(F32) + jnp.dot(
                left, right, preferred_element_type=F32
            )
            sums[t] = total.astype(BF16)
            return total

        unroll = 4 if steps % 4 == 0 else 1

        def several(t, total):
            for u in range(unroll):
                total = step(t * unroll + u, total)
            return total

        lax.fori_loop(0, steps // unroll, several, jnp.zeros((side, width), F32))

        def hand_out(b, _):
            for i in range(1, n_sec):
                first = lax.rem(sec + i, n_sec) * own_tiles + b * group
                for k in range(group):
                    agg_out[c, i - 1, b * group + k] = sums[plan[5, first + k]]
                agg_copy(c, i, b).start()
            return 0

        lax.fori_loop(0, groups, hand_out, 0)

        def keep_own(b, _):
            agg[b, :, pl.ds(pl.multiple_of(my_cols + c * width, 128), width)] = sums[
                plan[5, sec * own_tiles + b]
            ]
            return 0

        lax.fori_loop(0, own_tiles, keep_own, 0)

    loads[5].wait()
    own_feats.wait()

    def feat_in(i, _):
        feat_arrival(i).wait_recv()
        return 0

    lax.fori_loop(1, n_sec, feat_in, 0)

    def out_copies(b):
        rows = pl.ds(b * group, group)
        return (
            pltpu.make_async_copy(agg.at[rows], hidden_hbm.at[rows], out_sem.at[0, b]),
            pltpu.make_async_copy(target.at[rows], prev_hbm.at[rows], out_sem.at[1, b]),
        )

    def hidden_block(b, _):
        for c in range(chunks):
            for i in range(1, n_sec):
                agg_arrival(c, i, b).wait_recv()
        rows = pl.ds(b * group, group)
        values = agg[rows].reshape(group * side, d)
        hidden = jnp.tanh(
            jnp.dot(values, w_fwd[...], preferred_element_type=F32) + b_fwd[...]
        ).astype(BF16)
        agg[rows] = hidden.reshape(group, side, d)
        out_copies(b)[0].start()
        back = inverse(hidden).reshape(group, side, d)
        shifted = whole_feats[rows].astype(F32) + base[rows] - back
        target[rows] = shifted.astype(BF16)
        out_copies(b)[1].start()
        return 0

    lax.fori_loop(0, groups, hidden_block, 0)

    def finish(b, _):
        for copy in out_copies(b):
            copy.wait()
        for c in range(chunks):
            for i in range(1, n_sec):
                agg_copy(c, i, b).wait_send()
        return 0

    lax.fori_loop(0, groups, finish, 0)

    def sent_feat(i, _):
        feat_copy(i).wait_send()
        return 0

    lax.fori_loop(1, n_sec, sent_feat, 0)

    def sent_dom(i, _):
        for c in range(chunks):
            dom_copy(c, i).wait_send()
        return 0

    lax.fori_loop(0, n - 1, sent_dom, 0)


def per_device(
    n,
    n_sec,
    feats,
    tile_vals,
    src_slot,
    dst_tile,
    tile_count,
    send_tile,
    w_fwd,
    b_fwd,
    w_inv1,
    b_inv1,
    w_inv2,
    b_inv2,
    target,
):
    node_rows, cols = feats.shape
    entries, side, _ = tile_vals.shape
    row_tiles = node_rows // side
    own_tiles = row_tiles // n_sec
    slots = send_tile.shape[1] // n
    d = w_fwd.shape[0]
    width = 128 if cols % 128 == 0 else cols
    chunks = cols // width
    steps = (entries + row_tiles + 1) // 2
    steps = (steps + 3) // 4 * 4
    plan_width = (max(steps, row_tiles) + 127) // 128 * 128
    group = 2 if own_tiles % 2 == 0 else 1
    groups = own_tiles // group
    smem = pl.BlockSpec(memory_space=pltpu.SMEM)
    vmem = pl.BlockSpec(memory_space=pltpu.VMEM)
    hbm = pl.BlockSpec(memory_space=pl.ANY)

    plan = pl.pallas_call(
        functools.partial(plan_kernel, steps, row_tiles),
        out_shape=jax.ShapeDtypeStruct((8, plan_width), jnp.int32),
        in_specs=[smem, vmem, vmem],
        out_specs=vmem,
    )(tile_count, dst_tile.reshape(1, entries), src_slot.reshape(1, entries))

    cfg = (n, n_sec, slots, chunks, width, steps, group)
    rows_shape = (own_tiles, side, d)
    dma = pltpu.SemaphoreType.DMA
    scratch = [
        pltpu.VMEM((row_tiles, side, cols), BF16),
        pltpu.VMEM((entries + 1, side, side), BF16),
        pltpu.VMEM(rows_shape, BF16),
        pltpu.VMEM((d, d), BF16),
        pltpu.VMEM((d, d), BF16),
        pltpu.VMEM((d, d), BF16),
        pltpu.VMEM(rows_shape, BF16),
        pltpu.VMEM(rows_shape, F32),
        pltpu.VMEM(rows_shape, BF16),
        pltpu.VMEM((chunks, n_sec - 1, own_tiles, side, width), BF16),
        pltpu.VMEM((steps + 1, side, width), BF16),
        dma((7,)),
        dma((2, groups)),
        dma((chunks, n - 1)),
        dma((chunks, n - 1)),
        dma((n_sec,)),
        dma((n_sec,)),
        dma((chunks, n_sec, groups)),
        dma((chunks, n_sec, groups)),
    ]
    scratch += [pltpu.VMEM(((n - 1) * slots, side, width), BF16) for _ in range(chunks)]
    scratch += [pltpu.VMEM((n * slots, side, width), BF16) for _ in range(chunks)]
    hidden, prev = pl.pallas_call(
        functools.partial(layer_kernel, cfg),
        out_shape=[jax.ShapeDtypeStruct(rows_shape, BF16)] * 2,
        in_specs=[smem, smem] + [hbm] * 6 + [vmem] * 3,
        out_specs=[hbm, hbm],
        scratch_shapes=scratch,
        compiler_params=pltpu.CompilerParams(
            collective_id=0, has_side_effects=True, vmem_limit_bytes=63 * 1024 * 1024
        ),
    )(
        send_tile,
        plan,
        feats.reshape(row_tiles, side, cols),
        tile_vals,
        target.reshape(rows_shape),
        w_fwd,
        w_inv1,
        w_inv2,
        b_fwd.reshape(1, d),
        b_inv1.reshape(1, d),
        b_inv2.reshape(1, d),
    )
    return hidden.reshape(target.shape), prev.reshape(target.shape)


def solution(mesh):
    placed = (
        P("dom", "section"),
        P("dom", None, None),
        P("dom"),
        P("dom"),
        P("dom"),
        P("dom", None),
        P(),
        P(),
        P(),
        P(),
        P(),
        P(),
        P(("dom", "section"), None),
    )
    return jax.shard_map(
        functools.partial(per_device, mesh.shape["dom"], mesh.shape["section"]),
        mesh=mesh,
        in_specs=placed,
        out_specs=(P(("dom", "section"), None), P(("dom", "section"), None)),
        check_vma=False,
    )
```

time: 536 us -> 182 us (0.34)
  matrix products: 245 us -> 0 us
  Pallas kernels: 0 us -> 170 us
  waiting for transfers between devices: 161 us -> 0 us
  local copies, waits for them, and re-layouts: 88.9 us -> 6.83 us
  other arithmetic: 18.9 us -> 0 us
  starting transfers between devices: 18.1 us -> 0 us
    dot_general x49 -> x0, matrix products: 245 us -> none  [the longest x15 119 us: accumulate(): jnp.dot(place, products.reshape(BLOCK, flat_width), precision=lax.Precisi...]
    pallas_call x0 -> x2, Pallas kernels: none -> 170 us  [the longest x1 169 us: per_device(): pl.pallas_call(functools.partial(layer_kernel, cfg), out_shape=[jax.Shape...]
    all_to_all x3 -> x0, waiting for transfers between devices: 161 us -> none  [the longest x1 135 us: per_device(): lax.all_to_all(outgoing.reshape(recv_count, tile_side, feat_cols), 'dom',...]
    while x30 -> x0, local copies, waits for them, and re-layouts: 46.7 us -> none
    all_to_all x3 -> x0, starting transfers between devices: 18.1 us -> none  [the longest x1 6.61 us: per_device(): lax.all_to_all(outgoing.reshape(recv_count, tile_side, feat_cols), 'dom',...]
    convert_element_type x2 -> x0, local copies, waits for them, and re-layouts: 9.88 us -> none  [the longest x1 5.62 us: per_device(): agg = summed.reshape(node_rows, feat_cols).astype(jnp.bfloat16)]
    lt x15 -> x0, other arithmetic: 9.76 us -> none  [accumulate(): active = offset + jnp.arange(BLOCK, dtype=jnp.int32) < live_count]
    unnamed x16 -> x4, local copies, waits for them, and re-layouts: 14.3 us -> 6.83 us
  transfers between devices with their start and end apart: 3 -> 0, of which waited for: 2 -> 0; matrix products, arithmetic and copies ran while one was open for 57% -> 0% of each run, Pallas kernels for 0% -> 0%
where the time goes in v1:
time: 182 us; the launch traced here: 179 us
  Pallas kernels  170 us (93%)
  local copies, waits for them, and re-layouts  6.83 us (4%)
    pallas_call x1, Pallas kernels, per_device(): pl.pallas_call(functools.partial(layer_kernel, cfg), out_shape=[jax.Shape...  169 us
    unnamed x4, local copies, waits for them, and re-layouts  6.83 us

profile of v1, /device:TPU:9, one launch (start us, length us, event | category | flops | bytes accessed | tf_op | source)
XLA Modules:
  0.0 178.6 jit_solution(11790650000881075142)
XLA Ops:
  1.3 1.8 shard_map.140.plan
  3.0 168.7 %shard_map.141 = (bf16[16,128,1024]{2,1,0:T(8,128)(2,1)}, bf16[16,128,1024]{2,1,0:T(8,128)(2,1)}) custom-call(s32[1,48]{1,0:T(1,128)} %send_tile.1, s32[8,256]{1,0:T(8,128)} %shard_map.140.plan, bf16[32,128,512]{2,1,0:T(8,128)(2,1)} %bitcast.9, bf16[256,128,128]{2,1,0:T(8,128)(2,1)} %vals_hbm.1, bf16[16,128,1024]{2,1,0:T(8,128)(2,1)} %bitcast.10, ...), custom_call_target="tpu_custom_call" | custom-call | tf_op jit(solution)/shard_map/pallas_call | solution.py:441
  171.7 0.0 copy-start
  171.7 4.8 %copy.18 = bf16[2048,1024]{1,0:T(8,128)(2,1)} copy(bf16[2048,1024]{1,0:T(8,128)(2,1)} %bitcast.12) | data formatting | bytes 8388608
  176.6 0.0 copy-done
  176.6 2.0 %copy.19 = bf16[2048,1024]{1,0:T(8,128)(2,1)} copy(bf16[2048,1024]{1,0:T(8,128)(2,1)S(1)} %bitcast.11) | data formatting | bytes 8388608
Async XLA Ops:
  171.7 4.8 %copy-start = (bf16[16,128,1024]{2,1,0:T(8,128)(2,1)S(1)}, bf16[16,128,1024]{2,1,0:T(8,128)(2,1)}, u32[]{:S(2)}) copy-start(bf16[16,128,1024]{2,1,0:T(8,128)(2,1)} %get-tuple-element.5) | copy-start | bytes 12582916

commit v2 on v1

--- a/solution.py
+++ b/solution.py
@@ -81,7 +81,6 @@
     w_inv1,
     w_inv2,
     whole_feats,
-    base,
     agg,
     agg_out,
     sums,
@@ -114,8 +113,7 @@
         pltpu.make_async_copy(vals_hbm, vals.at[pl.ds(0, entries)], load_sem.at[4]),
         pltpu.make_async_copy(w_fwd_hbm, w_fwd, load_sem.at[5]),
     ]
-    for load in loads:
-        load.start()
+    loads[0].start()
 
     barrier = pltpu.get_barrier_semaphore()
 
@@ -238,6 +236,9 @@
             return 0
 
         lax.fori_loop(0, n - 1, send, 0)
+        if c == 0:
+            for load in loads[1:]:
+                load.start()
 
     def send_feat(i, _):
         feat_copy(i).start()
@@ -257,7 +258,7 @@
     def target_block(b, _):
         rows = pl.ds(b * group, group)
         values = target[rows].reshape(group * side, d)
-        base[rows] = inverse(values).reshape(group, side, d)
+        target[rows] = inverse(values).astype(BF16).reshape(group, side, d)
         return 0
 
     lax.fori_loop(0, groups, target_block, 0)
@@ -340,7 +341,7 @@
         agg[rows] = hidden.reshape(group, side, d)
         out_copies(b)[0].start()
         back = inverse(hidden).reshape(group, side, d)
-        shifted = whole_feats[rows].astype(F32) + base[rows] - back
+        shifted = whole_feats[rows].astype(F32) + target[rows].astype(F32) - back
         target[rows] = shifted.astype(BF16)
         out_copies(b)[1].start()
         return 0
@@ -394,7 +395,7 @@
     own_tiles = row_tiles // n_sec
     slots = send_tile.shape[1] // n
     d = w_fwd.shape[0]
-    width = 128 if cols % 128 == 0 else cols
+    width = 256 if cols % 256 == 0 else 128
     chunks = cols // width
     steps = (entries + row_tiles + 1) // 2
     steps = (steps + 3) // 4 * 4
@@ -423,7 +424,6 @@
         pltpu.VMEM((d, d), BF16),
         pltpu.VMEM((d, d), BF16),
         pltpu.VMEM(rows_shape, BF16),
-        pltpu.VMEM(rows_shape, F32),
         pltpu.VMEM(rows_shape, BF16),
         pltpu.VMEM((chunks, n_sec - 1, own_tiles, side, width), BF16),
         pltpu.VMEM((steps + 1, side, width), BF16),

time: 182 us -> 187 us (1.027)
  the two profiles are of different devices: /device:TPU:9 before, /device:TPU:13 now
where the time goes in v2:
time: 187 us
  Pallas kernels  179 us (96%)
  local copies, waits for them, and re-layouts  6.83 us (4%)
    pallas_call x1, Pallas kernels, per_device(): pl.pallas_call(functools.partial(layer_kernel, cfg), out_shape=[jax.Shape...  177 us
    unnamed x4, local copies, waits for them, and re-layouts  6.83 us

profile of v2, /device:TPU:13, one launch (start us, length us, event | category | flops | bytes accessed | tf_op | source)
XLA Modules:
  0.0 186.6 jit_solution(17822029654679165905)
XLA Ops:
  1.3 1.8 shard_map.140.plan
  3.0 176.8 %shard_map.141 = (bf16[16,128,1024]{2,1,0:T(8,128)(2,1)}, bf16[16,128,1024]{2,1,0:T(8,128)(2,1)}) custom-call(s32[1,48]{1,0:T(1,128)} %send_tile.1, s32[8,256]{1,0:T(8,128)} %shard_map.140.plan, bf16[32,128,512]{2,1,0:T(8,128)(2,1)} %bitcast.9, bf16[256,128,128]{2,1,0:T(8,128)(2,1)} %vals_hbm.1, bf16[16,128,1024]{2,1,0:T(8,128)(2,1)} %bitcast.10, ...), custom_call_target="tpu_custom_call" | custom-call | tf_op jit(solution)/shard_map/pallas_call | solution.py:441
  179.8 0.0 copy-start
  179.8 4.8 %copy.18 = bf16[2048,1024]{1,0:T(8,128)(2,1)} copy(bf16[2048,1024]{1,0:T(8,128)(2,1)} %bitcast.12) | data formatting | bytes 8388608
  184.6 0.0 copy-done
  184.6 2.0 %copy.19 = bf16[2048,1024]{1,0:T(8,128)(2,1)} copy(bf16[2048,1024]{1,0:T(8,128)(2,1)S(1)} %bitcast.11) | data formatting | bytes 8388608
Async XLA Ops:
  179.8 4.8 %copy-start = (bf16[16,128,1024]{2,1,0:T(8,128)(2,1)S(1)}, bf16[16,128,1024]{2,1,0:T(8,128)(2,1)}, u32[]{:S(2)}) copy-start(bf16[16,128,1024]{2,1,0:T(8,128)(2,1)} %get-tuple-element.5) | copy-start | bytes 12582916
